TPU v7x, 32 devices: a whole 2x2x4 slice. The times are simulated.
32 devices in a mesh: section: 4 (over y, x), dp: 8 (over z, core).
Axes of the slice: x: 2, y: 2, z: 4, core: 2. Of those that a mesh axis runs over, the one named last changes fastest.
Arguments:
- clean: bfloat16 [32, 16, 16, 384], P('dp'), may hold values from -12 to 12
- noise: bfloat16 [32, 16, 16, 384], P('dp'), may hold values from -6 to 6
- stamps: int32 [32], P('dp'), may hold values from 0 to 999
- enc_weight: bfloat16 [4, 3, 3, 384, 384], P('section'), may hold values from -0.109375 to 0.109375
- dec_weight: bfloat16 [4, 3, 3, 768, 384], P('section'), may hold values from -0.078125 to 0.078125
Outputs:
- enc_grad: float32 [4, 3, 3, 384, 384], P('section', None, None, 'dp')
- dec_grad: float32 [4, 3, 3, 768, 384], P('section', None, None, 'dp')
All inputs are finite; a program needn't handle non-finite values.
Results may differ from a plain program's by a relative error of at most 0.0035.
Values sent between devices are 32-bit elements; how exact they have to be, the bound alone decides.
No kernel may reach another device: no remote copies, remote signals or barrier semaphores. Data moves between devices by JAX's collectives and lax.ppermute only.
A program may use at most 128 MiB of HBM per device.

v0:
```python
import math

import jax
import jax.numpy as jnp
from jax import lax
from jax.sharding import PartitionSpec as P

GROUPS = 32


def passed_along(value, axis, steps):
    count = lax.axis_size(axis)
    initial, last = (max(0, -steps), min(count, count - steps))
    return lax.ppermute(value, axis, [(source, source + steps) for source in range(initial, last)])


def embed(stamps_in, channels):
    half_width = channels // 2
    frequency = jnp.exp(-math.log(10000.0) * jnp.arange(half_width, dtype=jnp.float32) / half_width)
    angles = stamps_in.astype(jnp.float32)[:, None] * frequency[None, :]
    return jnp.concatenate([jnp.sin(angles), jnp.cos(angles)], axis=1)


def activate(inputs_f32, stamps_in):
    batch_rows, height, breadth, channels = inputs_f32.shape
    grouped = inputs_f32.reshape(batch_rows, height * breadth, GROUPS, channels // GROUPS)
    group_mean = jnp.mean(grouped, axis=(1, 3), keepdims=True)
    centered = grouped - group_mean
    group_var = jnp.mean(centered * centered, axis=(1, 3), keepdims=True)
    normed = (centered * lax.rsqrt(group_var + 1e-05)).reshape(inputs_f32.shape)
    modulate = 1.0 + 0.5 * embed(stamps_in, channels)[:, None, None, :]
    return jax.nn.silu(normed * modulate)


def conv_apply(activations, weight):
    batch_rows, height, breadth, channels = activations.shape
    padded = jnp.pad(activations, ((0, 0), (1, 1), (1, 1), (0, 0)))
    summed = jnp.zeros((batch_rows * height * breadth, weight.shape[3]), jnp.float32)
    for row_off in range(3):
        for col_off in range(3):
            window = padded[:, row_off : row_off + height, col_off : col_off + breadth, :].reshape(
                -1, channels
            )
            summed = summed + jnp.dot(
                window, weight[row_off, col_off], preferred_element_type=jnp.float32
            )
    return summed.reshape(batch_rows, height, breadth, weight.shape[3])


def conv_back(cotangent, weight):
    batch_rows, height, breadth, outputs = cotangent.shape
    padded = jnp.pad(cotangent.astype(jnp.bfloat16), ((0, 0), (1, 1), (1, 1), (0, 0)))
    summed = jnp.zeros((batch_rows * height * breadth, weight.shape[2]), jnp.float32)
    for row_off in range(3):
        for col_off in range(3):
            window = padded[
                :, 2 - row_off : 2 - row_off + height, 2 - col_off : 2 - col_off + breadth, :
            ].reshape(-1, outputs)
            summed = summed + lax.dot_general(
                window,
                weight[row_off, col_off],
                (((1,), (1,)), ((), ())),
                preferred_element_type=jnp.float32,
            )
    return summed.reshape(batch_rows, height, breadth, weight.shape[2])


def conv_weight_grad(activations, cotangent):
    batch_rows, height, breadth, channels = activations.shape
    padded = jnp.pad(activations, ((0, 0), (1, 1), (1, 1), (0, 0)))
    flat_cot = cotangent.astype(jnp.bfloat16).reshape(-1, cotangent.shape[3])
    kernel_rows = []
    for row_off in range(3):
        kernel_cols = []
        for col_off in range(3):
            window = padded[:, row_off : row_off + height, col_off : col_off + breadth, :].reshape(
                -1, channels
            )
            kernel_cols.append(
                lax.dot_general(
                    window, flat_cot, (((0,), (0,)), ((), ())), preferred_element_type=jnp.float32
                )
            )
        kernel_rows.append(jnp.stack(kernel_cols))
    return jnp.stack(kernel_rows)


def block_forward(inputs, residual, weight, stamps_in):
    activations = activate(inputs, stamps_in).astype(jnp.bfloat16)
    return residual + conv_apply(activations, weight)


def block_backward(inputs, weight, stamps_in, cotangent):
    activated, pullback = jax.vjp(lambda inner_field: activate(inner_field, stamps_in), inputs)
    activations = activated.astype(jnp.bfloat16)
    weight_grad = conv_weight_grad(activations, cotangent)
    input_grad = pullback(conv_back(cotangent, weight))[0]
    return (input_grad, weight_grad)


def noise_levels(stamps_in):
    phase = (stamps_in.astype(jnp.float32) / 1000.0 + 0.008) / 1.008 * (math.pi / 2.0)
    signal = jnp.cos(phase) ** 2
    return (jnp.sqrt(signal), jnp.sqrt(1.0 - signal))


def pick_row(buffer, slot_index):
    return lax.dynamic_slice_in_dim(buffer, slot_index, 1, 0)


def store_row(buffer, piece, slot_index, active):
    kept = pick_row(buffer, slot_index)
    return lax.dynamic_update_slice_in_dim(buffer, jnp.where(active, piece, kept), slot_index, 0)


def shards(clean, noise, stamps, enc_weight, dec_weight):
    sections = lax.axis_size("section")
    section_index = lax.axis_index("section")
    last_section = sections - 1
    samples = clean.shape[0]
    channels = clean.shape[3]
    enc_kernel = enc_weight[0]
    dec_kernel = dec_weight[0]
    keep_level, spread_level = noise_levels(stamps)
    noisy = keep_level[:, None, None, None] * clean.astype(jnp.float32) + spread_level[
        :, None, None, None
    ] * noise.astype(jnp.float32)
    factor = 1.0 / math.sqrt(samples * lax.axis_size("dp") * clean.shape[1] * clean.shape[2])
    ticks_total = samples + sections - 1
    blank_piece = jnp.zeros((1,) + clean.shape[1:], jnp.float32)
    blank_buffer = jnp.zeros(clean.shape, jnp.float32)

    def locate(tick_now, offset):
        sample_id = tick_now - offset
        active = (sample_id >= 0) & (sample_id < samples)
        slot_index = jnp.clip(sample_id, 0, samples - 1)
        return (active, slot_index)

    def encoder_tick(tick_now, carried):
        incoming, enc_inputs, skips = carried
        active, slot_index = locate(tick_now, section_index)
        source = jnp.where(section_index == 0, pick_row(noisy, slot_index), incoming)
        stamp_one = pick_row(stamps, slot_index)
        result = lax.cond(
            active,
            lambda: block_forward(source, source, enc_kernel, stamp_one),
            lambda: blank_piece,
        )
        enc_inputs = store_row(enc_inputs, source, slot_index, active)
        skips = store_row(skips, result, slot_index, active)
        incoming = passed_along(result, "section", 1)
        return (incoming, enc_inputs, skips)

    _, enc_inputs, skips = lax.fori_loop(
        0, ticks_total, encoder_tick, (blank_piece, blank_buffer, blank_buffer)
    )

    def decoder_tick(tick_now, carried):
        incoming, dec_inputs, outputs = carried
        active, slot_index = locate(tick_now, last_section - section_index)
        skip_piece = pick_row(skips, slot_index)
        source = jnp.where(section_index == last_section, skip_piece, incoming)
        joined = jnp.concatenate([source, skip_piece], axis=3)
        stamp_one = pick_row(stamps, slot_index)
        result = lax.cond(
            active,
            lambda: block_forward(joined, source, dec_kernel, stamp_one),
            lambda: blank_piece,
        )
        dec_inputs = store_row(dec_inputs, source, slot_index, active)
        outputs = store_row(outputs, result, slot_index, active)
        incoming = passed_along(result, "section", -1)
        return (incoming, dec_inputs, outputs)

    _, dec_inputs, outputs = lax.fori_loop(
        0, ticks_total, decoder_tick, (blank_piece, blank_buffer, blank_buffer)
    )

    def decoder_back_tick(tick_now, carried):
        incoming, dec_acc, skip_grads, up_grads = carried
        active, slot_index = locate(tick_now, section_index)
        top_grad = factor * (
            pick_row(outputs, slot_index) - pick_row(noise, slot_index).astype(jnp.float32)
        )
        flowing = jnp.where(section_index == 0, top_grad, incoming)
        joined = jnp.concatenate(
            [pick_row(dec_inputs, slot_index), pick_row(skips, slot_index)], axis=3
        )
        stamp_one = pick_row(stamps, slot_index)

        def decoder_working(accum):
            input_grad, weight_grad = block_backward(joined, dec_kernel, stamp_one, flowing)
            up_piece = input_grad[..., :channels] + flowing
            return (accum + weight_grad, up_piece, input_grad[..., channels:])

        def decoder_resting(accum):
            return (accum, blank_piece, blank_piece)

        dec_acc, up_piece, skip_grad = lax.cond(active, decoder_working, decoder_resting, dec_acc)
        skip_grads = store_row(skip_grads, skip_grad, slot_index, active)
        up_grads = store_row(up_grads, up_piece, slot_index, active)
        incoming = passed_along(up_piece, "section", 1)
        return (incoming, dec_acc, skip_grads, up_grads)

    dec_start = jnp.zeros(dec_kernel.shape, jnp.float32)
    _, dec_acc, skip_grads, up_grads = lax.fori_loop(
        0, ticks_total, decoder_back_tick, (blank_piece, dec_start, blank_buffer, blank_buffer)
    )

    def encoder_back_tick(tick_now, carried):
        incoming, enc_acc = carried
        active, slot_index = locate(tick_now, last_section - section_index)
        arriving = jnp.where(
            section_index == last_section, pick_row(up_grads, slot_index), incoming
        )
        merged = arriving + pick_row(skip_grads, slot_index)
        block_input = pick_row(enc_inputs, slot_index)
        stamp_one = pick_row(stamps, slot_index)

        def encoder_working(accum):
            input_grad, weight_grad = block_backward(block_input, enc_kernel, stamp_one, merged)
            return (accum + weight_grad, input_grad + merged)

        def encoder_resting(accum):
            return (accum, blank_piece)

        enc_acc, down_piece = lax.cond(active, encoder_working, encoder_resting, enc_acc)
        incoming = passed_along(down_piece, "section", -1)
        return (incoming, enc_acc)

    enc_start = jnp.zeros(enc_kernel.shape, jnp.float32)
    _, enc_acc = lax.fori_loop(0, ticks_total, encoder_back_tick, (blank_piece, enc_start))
    enc_share, dec_share = (
        lax.psum_scatter(enc_acc[None], "dp", scatter_dimension=3, tiled=True),
        lax.psum_scatter(dec_acc[None], "dp", scatter_dimension=3, tiled=True),
    )
    return (enc_share, dec_share)


def solution(mesh):
    placed = (
        P("dp", None, None, None),
        P("dp", None, None, None),
        P("dp"),
        P("section", None, None, None, None),
        P("section", None, None, None, None),
    )
    return jax.shard_map(
        shards,
        mesh=mesh,
        in_specs=placed,
        out_specs=(P("section", None, None, "dp", None), P("section", None, None, "dp", None)),
        check_vma=False,
    )
```

profile of v0, /device:TPU:0, one launch (start us, length us, event | category | flops | bytes accessed | tf_op | source)
XLA Modules:
  0.0 976.2 jit_solution(104590118792861301)
XLA Ops:
  14.3 124.2 %while.80 = (s32[]{:T(128)}, f32[1,16,16,384]{3,2,1,0:T(8,128)}, f32[4,16,16,384]{3,2,1,0:T(8,128)}, f32[4,16,16,384]{3,2,1,0:T(8,128)}, s32[]{:T(128)}, /*index...) while((s32[]{:T(128)}, f32[1,16,16,384]{3,2,1,0:T(8,128)}, ...), condition=%wide.region_7.8_spmd, body=%wide.region_0.7_spmd.sunk | while | flops 681838080 | bytes 20187440 | solution.py:154
  91.9 10.7 %collective-permute-start = (f32[1,16,16,384]{3,2,1,0:T(8,128)S(1)}, f32[1,16,16,384]{3,2,1,0:T(8,128)}, u32[]{:S(2)}, u32[]{:S(2)}) collective-permute-start(f32[1,16,16,384]{3,2,1,0:T(8,128)S(1)} %get-tuple-element.1695), channel_id=1, source_target_pairs={{0,8},{8,16},{16,24},{1,9},{9,17},{17,25},{2,10},{10,18},{18,26},{... | collective-permute-start | bytes 1179656 | tf_op jit(solution)/shard_map/while/body/eval_jaxpr/ppermute | solution.py:14
  122.6 11.5 %collective-permute-start = (f32[1,16,16,384]{3,2,1,0:T(8,128)S(1)}, f32[1,16,16,384]{3,2,1,0:T(8,128)}, u32[]{:S(2)}, u32[]{:S(2)}) collective-permute-start(f32[1,16,16,384]{3,2,1,0:T(8,128)S(1)} %get-tuple-element.1695), channel_id=1, source_target_pairs={{0,8},{8,16},{16,24},{1,9},{9,17},{17,25},{2,10},{10,18},{18,26},{... | collective-permute-start | bytes 1179656 | tf_op jit(solution)/shard_map/while/body/eval_jaxpr/ppermute | solution.py:14
  141.2 144.8 %while.81 = (s32[]{:T(128)}, f32[1,16,16,384]{3,2,1,0:T(8,128)S(1)}, f32[4,16,16,384]{3,2,1,0:T(8,128)}, f32[4,16,16,384]{3,2,1,0:T(8,128)}, s32[]{:T(128)}, /*i...) while((s32[]{:T(128)}, ...), condition=%wide.region_15.16_spmd, body=%wide.region_8.15_spmd.sunk | while | flops 1362693120 | bytes 50988884 | solution.py:175
  173.9 30.4 %collective-permute-done.1 = f32[1,16,16,384]{3,2,1,0:T(8,128)S(1)} collective-permute-done((f32[1,16,16,384]{3,2,1,0:T(8,128)S(1)}, f32[1,16,16,384]{3,2,1,0:T(8,128)S(1)}, u32[]{:S(2)}, u32[]{:S(2)}) %collective-permute-start.1) | collective-permute-done | bytes 393248 | tf_op jit(solution)/shard_map/while/body/eval_jaxpr/ppermute | solution.py:14
  293.5 248.1 %while.82 = (s32[]{:T(128)}, f32[1,16,16,384]{3,2,1,0:T(8,128)S(1)}, f32[3,3,768,384]{3,2,1,0:T(8,128)}, f32[4,16,16,384]{3,2,1,0:T(8,128)}, f32[4,16,16,384]{3,...) while((s32[]{:T(128)}, ...), condition=%wide.region_27.28_spmd, body=%wide.region_16.27_spmd.sunk | while | flops 2744945920 | bytes 206576816 | solution.py:206
  296.9 26.6 %conditional.10 = (f32[3,3,768,384]{3,2,1,0:T(8,128)}, f32[1,16,16,384]{3,2,1,0:T(8,128)S(1)}, f32[1,16,16,384]{3,2,1,0:T(8,128)}) conditional(s32[]{:T(128)} %convert_element_type.139, f32[3,3,768,384]{3,2,1,0:T(8,128)} %get-tuple-element.1624, (f32[1,16,16,768]{3,2,1,0:T(8,128)S(1)}, s32[4]{0:T(128)S(1)}, s32[]{:T(128)}, pred[]{:T(512)}, ...), branch_computations={%region_17.17_spmd, %region_18.26_spmd} | conditional | flops 2744454400 | bytes 198908256 | solution.py:199
  333.1 26.6 %conditional.10 = (f32[3,3,768,384]{3,2,1,0:T(8,128)}, f32[1,16,16,384]{3,2,1,0:T(8,128)S(1)}, f32[1,16,16,384]{3,2,1,0:T(8,128)}) conditional(s32[]{:T(128)} %convert_element_type.139, f32[3,3,768,384]{3,2,1,0:T(8,128)} %get-tuple-element.1624, (f32[1,16,16,768]{3,2,1,0:T(8,128)S(1)}, s32[4]{0:T(128)S(1)}, s32[]{:T(128)}, pred[]{:T(512)}, ...), branch_computations={%region_17.17_spmd, %region_18.26_spmd} | conditional | flops 2744454400 | bytes 198908256 | solution.py:199
  372.5 26.6 %conditional.10 = (f32[3,3,768,384]{3,2,1,0:T(8,128)}, f32[1,16,16,384]{3,2,1,0:T(8,128)S(1)}, f32[1,16,16,384]{3,2,1,0:T(8,128)}) conditional(s32[]{:T(128)} %convert_element_type.139, f32[3,3,768,384]{3,2,1,0:T(8,128)} %get-tuple-element.1624, (f32[1,16,16,768]{3,2,1,0:T(8,128)S(1)}, s32[4]{0:T(128)S(1)}, s32[]{:T(128)}, pred[]{:T(512)}, ...), branch_computations={%region_17.17_spmd, %region_18.26_spmd} | conditional | flops 2744454400 | bytes 198908256 | solution.py:199
  411.9 26.6 %conditional.10 = (f32[3,3,768,384]{3,2,1,0:T(8,128)}, f32[1,16,16,384]{3,2,1,0:T(8,128)S(1)}, f32[1,16,16,384]{3,2,1,0:T(8,128)}) conditional(s32[]{:T(128)} %convert_element_type.139, f32[3,3,768,384]{3,2,1,0:T(8,128)} %get-tuple-element.1624, (f32[1,16,16,768]{3,2,1,0:T(8,128)S(1)}, s32[4]{0:T(128)S(1)}, s32[]{:T(128)}, pred[]{:T(512)}, ...), branch_computations={%region_17.17_spmd, %region_18.26_spmd} | conditional | flops 2744454400 | bytes 198908256 | solution.py:199
  452.1 30.2 %collective-permute-start.2 = (f32[1,16,16,384]{3,2,1,0:T(8,128)S(1)}, f32[1,16,16,384]{3,2,1,0:T(8,128)S(1)}, u32[]{:S(2)}, u32[]{:S(2)}) collective-permute-start(f32[1,16,16,384]{3,2,1,0:T(8,128)S(1)} %get-tuple-element.1500), channel_id=1, source_target_pairs={{0,8},{8,16},{16,24},{1,9},{9,17},{17,25},{2,10},{10,18},{18,26},{... | collective-permute-start | bytes 1179656 | tf_op jit(solution)/shard_map/while/body/eval_jaxpr/ppermute | solution.py:14
  505.3 31.1 %collective-permute-start.2 = (f32[1,16,16,384]{3,2,1,0:T(8,128)S(1)}, f32[1,16,16,384]{3,2,1,0:T(8,128)S(1)}, u32[]{:S(2)}, u32[]{:S(2)}) collective-permute-start(f32[1,16,16,384]{3,2,1,0:T(8,128)S(1)} %get-tuple-element.1500), channel_id=1, source_target_pairs={{0,8},{8,16},{16,24},{1,9},{9,17},{17,25},{2,10},{10,18},{18,26},{... | collective-permute-start | bytes 1179656 | tf_op jit(solution)/shard_map/while/body/eval_jaxpr/ppermute | solution.py:14
  544.5 254.7 %while.83 = (s32[]{:T(128)}, f32[1,16,16,384]{3,2,1,0:T(8,128)S(1)}, f32[3,3,384,384]{3,2,1,0:T(8,128)}, s32[]{:T(128)}, f32[4,16,16,384]{3,2,1,0:T(8,128)}, /*i...) while((s32[]{:T(128)}, ...), condition=%wide.region_39.40_spmd, body=%wide.region_28.39_spmd.sunk | while | flops 1370015488 | bytes 93357616 | solution.py:232
  546.8 9.9 %collective-permute-done.3 = f32[1,16,16,384]{3,2,1,0:T(8,128)S(1)} collective-permute-done((f32[1,16,16,384]{3,2,1,0:T(8,128)}, f32[1,16,16,384]{3,2,1,0:T(8,128)S(1)}, u32[]{:S(2)}, u32[]{:S(2)}) %collective-permute-start.3) | collective-permute-done | bytes 393248 | tf_op jit(solution)/shard_map/while/body/eval_jaxpr/ppermute | solution.py:14
  558.9 31.5 %collective-permute-done.3 = f32[1,16,16,384]{3,2,1,0:T(8,128)S(1)} collective-permute-done((f32[1,16,16,384]{3,2,1,0:T(8,128)}, f32[1,16,16,384]{3,2,1,0:T(8,128)S(1)}, u32[]{:S(2)}, u32[]{:S(2)}) %collective-permute-start.3) | collective-permute-done | bytes 393248 | tf_op jit(solution)/shard_map/while/body/eval_jaxpr/ppermute | solution.py:14
  592.4 74.1 %collective-permute-done.3 = f32[1,16,16,384]{3,2,1,0:T(8,128)S(1)} collective-permute-done((f32[1,16,16,384]{3,2,1,0:T(8,128)}, f32[1,16,16,384]{3,2,1,0:T(8,128)S(1)}, u32[]{:S(2)}, u32[]{:S(2)}) %collective-permute-start.3) | collective-permute-done | bytes 393248 | tf_op jit(solution)/shard_map/while/body/eval_jaxpr/ppermute | solution.py:14
  666.4 22.7 %conditional.11 = (f32[3,3,384,384]{3,2,1,0:T(8,128)}, f32[1,16,16,384]{3,2,1,0:T(8,128)}) conditional(s32[]{:T(128)} %convert_element_type.140, f32[3,3,384,384]{3,2,1,0:T(8,128)} %get-tuple-element.1671, (s32[]{:T(128)}, f32[4,16,16,384]{3,2,1,0:T(8,128)}, s32[4]{0:T(128)S(1)}, pred[]{:T(512)}, f32[4,16,16,384]{3,2,1,0:T(8,128)}, ...), branch_computations={%region_29.29_spmd, %region_30.38_spmd} | conditional | flops 1370015488 | bytes 91784480 | solution.py:227
  690.4 9.5 collective-permute-done.3
  699.9 22.7 %conditional.11 = (f32[3,3,384,384]{3,2,1,0:T(8,128)}, f32[1,16,16,384]{3,2,1,0:T(8,128)}) conditional(s32[]{:T(128)} %convert_element_type.140, f32[3,3,384,384]{3,2,1,0:T(8,128)} %get-tuple-element.1671, (s32[]{:T(128)}, f32[4,16,16,384]{3,2,1,0:T(8,128)}, s32[4]{0:T(128)S(1)}, pred[]{:T(512)}, f32[4,16,16,384]{3,2,1,0:T(8,128)}, ...), branch_computations={%region_29.29_spmd, %region_30.38_spmd} | conditional | flops 1370015488 | bytes 91784480 | solution.py:227
  723.8 9.5 collective-permute-done.3
  733.3 22.7 %conditional.11 = (f32[3,3,384,384]{3,2,1,0:T(8,128)}, f32[1,16,16,384]{3,2,1,0:T(8,128)}) conditional(s32[]{:T(128)} %convert_element_type.140, f32[3,3,384,384]{3,2,1,0:T(8,128)} %get-tuple-element.1671, (s32[]{:T(128)}, f32[4,16,16,384]{3,2,1,0:T(8,128)}, s32[4]{0:T(128)S(1)}, pred[]{:T(512)}, f32[4,16,16,384]{3,2,1,0:T(8,128)}, ...), branch_computations={%region_29.29_spmd, %region_30.38_spmd} | conditional | flops 1370015488 | bytes 91784480 | solution.py:227
  766.7 22.7 %conditional.11 = (f32[3,3,384,384]{3,2,1,0:T(8,128)}, f32[1,16,16,384]{3,2,1,0:T(8,128)}) conditional(s32[]{:T(128)} %convert_element_type.140, f32[3,3,384,384]{3,2,1,0:T(8,128)} %get-tuple-element.1671, (s32[]{:T(128)}, f32[4,16,16,384]{3,2,1,0:T(8,128)}, s32[4]{0:T(128)S(1)}, pred[]{:T(512)}, f32[4,16,16,384]{3,2,1,0:T(8,128)}, ...), branch_computations={%region_29.29_spmd, %region_30.38_spmd} | conditional | flops 1370015488 | bytes 91784480 | solution.py:227
  800.0 57.5 %reduce-scatter.3.cloned.1.call-done = f32[1,3,3,48,384]{4,3,2,1,0:T(8,128)} async-done(((f32[1,3,3,384,384]{4,3,2,1,0:T(8,128)}), f32[1,3,3,48,384]{4,3,2,1,0:T(8,128)}) %reduce-scatter.3.cloned.1.call-update) | async-done | bytes 663568 | tf_op jit(solution)/shard_map/reduce_scatter | solution.py:234
  857.5 111.9 %reduce-scatter.5.cloned.1.call-done = f32[1,3,3,96,384]{4,3,2,1,0:T(8,128)} async-done(((f32[1,3,3,768,384]{4,3,2,1,0:T(8,128)}), f32[1,3,3,96,384]{4,3,2,1,0:T(8,128)}) %reduce-scatter.5.cloned.1.call-update) | async-done | bytes 1327120 | tf_op jit(solution)/shard_map/reduce_scatter | solution.py:235
  (891 shorter events, 588.0 us)
Async XLA Ops:
  7.2 850.3 %reduce-scatter.3.cloned.1.call-start = ((), (), s32[]{:S(2)}) async-start(), calls=%async_computation.2 | async-start | bytes 5971968 | tf_op jit(solution)/shard_map/reduce_scatter | solution.py:234
  21.5 10.6 %collective-permute-start = (f32[1,16,16,384]{3,2,1,0:T(8,128)S(1)}, f32[1,16,16,384]{3,2,1,0:T(8,128)}, u32[]{:S(2)}, u32[]{:S(2)}) collective-permute-start(f32[1,16,16,384]{3,2,1,0:T(8,128)S(1)} %get-tuple-element.1695), channel_id=1, source_target_pairs={{0,8},{8,16},{16,24},{1,9},{9,17},{17,25},{2,10},{10,18},{18,26},{... | collective-permute-start | bytes 1179656 | tf_op jit(solution)/shard_map/while/body/eval_jaxpr/ppermute | solution.py:14
  39.2 13.0 %collective-permute-start = (f32[1,16,16,384]{3,2,1,0:T(8,128)S(1)}, f32[1,16,16,384]{3,2,1,0:T(8,128)}, u32[]{:S(2)}, u32[]{:S(2)}) collective-permute-start(f32[1,16,16,384]{3,2,1,0:T(8,128)S(1)} %get-tuple-element.1695), channel_id=1, source_target_pairs={{0,8},{8,16},{16,24},{1,9},{9,17},{17,25},{2,10},{10,18},{18,26},{... | collective-permute-start | bytes 1179656 | tf_op jit(solution)/shard_map/while/body/eval_jaxpr/ppermute | solution.py:14
  59.4 12.1 %collective-permute-start = (f32[1,16,16,384]{3,2,1,0:T(8,128)S(1)}, f32[1,16,16,384]{3,2,1,0:T(8,128)}, u32[]{:S(2)}, u32[]{:S(2)}) collective-permute-start(f32[1,16,16,384]{3,2,1,0:T(8,128)S(1)} %get-tuple-element.1695), channel_id=1, source_target_pairs={{0,8},{8,16},{16,24},{1,9},{9,17},{17,25},{2,10},{10,18},{18,26},{... | collective-permute-start | bytes 1179656 | tf_op jit(solution)/shard_map/while/body/eval_jaxpr/ppermute | solution.py:14
  78.7 11.2 %collective-permute-start = (f32[1,16,16,384]{3,2,1,0:T(8,128)S(1)}, f32[1,16,16,384]{3,2,1,0:T(8,128)}, u32[]{:S(2)}, u32[]{:S(2)}) collective-permute-start(f32[1,16,16,384]{3,2,1,0:T(8,128)S(1)} %get-tuple-element.1695), channel_id=1, source_target_pairs={{0,8},{8,16},{16,24},{1,9},{9,17},{17,25},{2,10},{10,18},{18,26},{... | collective-permute-start | bytes 1179656 | tf_op jit(solution)/shard_map/while/body/eval_jaxpr/ppermute | solution.py:14
  91.9 15.9 %collective-permute-start = (f32[1,16,16,384]{3,2,1,0:T(8,128)S(1)}, f32[1,16,16,384]{3,2,1,0:T(8,128)}, u32[]{:S(2)}, u32[]{:S(2)}) collective-permute-start(f32[1,16,16,384]{3,2,1,0:T(8,128)S(1)} %get-tuple-element.1695), channel_id=1, source_target_pairs={{0,8},{8,16},{16,24},{1,9},{9,17},{17,25},{2,10},{10,18},{18,26},{... | collective-permute-start | bytes 1179656 | tf_op jit(solution)/shard_map/while/body/eval_jaxpr/ppermute | solution.py:14
  109.8 10.8 %collective-permute-start = (f32[1,16,16,384]{3,2,1,0:T(8,128)S(1)}, f32[1,16,16,384]{3,2,1,0:T(8,128)}, u32[]{:S(2)}, u32[]{:S(2)}) collective-permute-start(f32[1,16,16,384]{3,2,1,0:T(8,128)S(1)} %get-tuple-element.1695), channel_id=1, source_target_pairs={{0,8},{8,16},{16,24},{1,9},{9,17},{17,25},{2,10},{10,18},{18,26},{... | collective-permute-start | bytes 1179656 | tf_op jit(solution)/shard_map/while/body/eval_jaxpr/ppermute | solution.py:14
  122.6 16.0 %collective-permute-start = (f32[1,16,16,384]{3,2,1,0:T(8,128)S(1)}, f32[1,16,16,384]{3,2,1,0:T(8,128)}, u32[]{:S(2)}, u32[]{:S(2)}) collective-permute-start(f32[1,16,16,384]{3,2,1,0:T(8,128)S(1)} %get-tuple-element.1695), channel_id=1, source_target_pairs={{0,8},{8,16},{16,24},{1,9},{9,17},{17,25},{2,10},{10,18},{18,26},{... | collective-permute-start | bytes 1179656 | tf_op jit(solution)/shard_map/while/body/eval_jaxpr/ppermute | solution.py:14
  143.4 11.1 %collective-permute-start.1 = (f32[1,16,16,384]{3,2,1,0:T(8,128)S(1)}, f32[1,16,16,384]{3,2,1,0:T(8,128)S(1)}, u32[]{:S(2)}, u32[]{:S(2)}) collective-permute-start(f32[1,16,16,384]{3,2,1,0:T(8,128)S(1)} %get-tuple-element.1696), channel_id=1, source_target_pairs={{8,0},{16,8},{24,16},{9,1},{17,9},{25,17},{10,2},{18,10},{26,18},{... | collective-permute-start | bytes 1179656 | tf_op jit(solution)/shard_map/while/body/eval_jaxpr/ppermute | solution.py:14
  156.7 12.0 %collective-permute-start.1 = (f32[1,16,16,384]{3,2,1,0:T(8,128)S(1)}, f32[1,16,16,384]{3,2,1,0:T(8,128)S(1)}, u32[]{:S(2)}, u32[]{:S(2)}) collective-permute-start(f32[1,16,16,384]{3,2,1,0:T(8,128)S(1)} %get-tuple-element.1696), channel_id=1, source_target_pairs={{8,0},{16,8},{24,16},{9,1},{17,9},{25,17},{10,2},{18,10},{26,18},{... | collective-permute-start | bytes 1179656 | tf_op jit(solution)/shard_map/while/body/eval_jaxpr/ppermute | solution.py:14
  170.8 33.5 %collective-permute-start.1 = (f32[1,16,16,384]{3,2,1,0:T(8,128)S(1)}, f32[1,16,16,384]{3,2,1,0:T(8,128)S(1)}, u32[]{:S(2)}, u32[]{:S(2)}) collective-permute-start(f32[1,16,16,384]{3,2,1,0:T(8,128)S(1)} %get-tuple-element.1696), channel_id=1, source_target_pairs={{8,0},{16,8},{24,16},{9,1},{17,9},{25,17},{10,2},{18,10},{26,18},{... | collective-permute-start | bytes 1179656 | tf_op jit(solution)/shard_map/while/body/eval_jaxpr/ppermute | solution.py:14
  214.4 10.6 %collective-permute-start.1 = (f32[1,16,16,384]{3,2,1,0:T(8,128)S(1)}, f32[1,16,16,384]{3,2,1,0:T(8,128)S(1)}, u32[]{:S(2)}, u32[]{:S(2)}) collective-permute-start(f32[1,16,16,384]{3,2,1,0:T(8,128)S(1)} %get-tuple-element.1696), channel_id=1, source_target_pairs={{8,0},{16,8},{24,16},{9,1},{17,9},{25,17},{10,2},{18,10},{26,18},{... | collective-permute-start | bytes 1179656 | tf_op jit(solution)/shard_map/while/body/eval_jaxpr/ppermute | solution.py:14
  235.1 10.6 %collective-permute-start.1 = (f32[1,16,16,384]{3,2,1,0:T(8,128)S(1)}, f32[1,16,16,384]{3,2,1,0:T(8,128)S(1)}, u32[]{:S(2)}, u32[]{:S(2)}) collective-permute-start(f32[1,16,16,384]{3,2,1,0:T(8,128)S(1)} %get-tuple-element.1696), channel_id=1, source_target_pairs={{8,0},{16,8},{24,16},{9,1},{17,9},{25,17},{10,2},{18,10},{26,18},{... | collective-permute-start | bytes 1179656 | tf_op jit(solution)/shard_map/while/body/eval_jaxpr/ppermute | solution.py:14
  255.7 10.6 %collective-permute-start.1 = (f32[1,16,16,384]{3,2,1,0:T(8,128)S(1)}, f32[1,16,16,384]{3,2,1,0:T(8,128)S(1)}, u32[]{:S(2)}, u32[]{:S(2)}) collective-permute-start(f32[1,16,16,384]{3,2,1,0:T(8,128)S(1)} %get-tuple-element.1696), channel_id=1, source_target_pairs={{8,0},{16,8},{24,16},{9,1},{17,9},{25,17},{10,2},{18,10},{26,18},{... | collective-permute-start | bytes 1179656 | tf_op jit(solution)/shard_map/while/body/eval_jaxpr/ppermute | solution.py:14
  452.1 35.4 %collective-permute-start.2 = (f32[1,16,16,384]{3,2,1,0:T(8,128)S(1)}, f32[1,16,16,384]{3,2,1,0:T(8,128)S(1)}, u32[]{:S(2)}, u32[]{:S(2)}) collective-permute-start(f32[1,16,16,384]{3,2,1,0:T(8,128)S(1)} %get-tuple-element.1500), channel_id=1, source_target_pairs={{0,8},{8,16},{16,24},{1,9},{9,17},{17,25},{2,10},{10,18},{18,26},{... | collective-permute-start | bytes 1179656 | tf_op jit(solution)/shard_map/while/body/eval_jaxpr/ppermute | solution.py:14
  491.5 9.9 %collective-permute-start.2 = (f32[1,16,16,384]{3,2,1,0:T(8,128)S(1)}, f32[1,16,16,384]{3,2,1,0:T(8,128)S(1)}, u32[]{:S(2)}, u32[]{:S(2)}) collective-permute-start(f32[1,16,16,384]{3,2,1,0:T(8,128)S(1)} %get-tuple-element.1500), channel_id=1, source_target_pairs={{0,8},{8,16},{16,24},{1,9},{9,17},{17,25},{2,10},{10,18},{18,26},{... | collective-permute-start | bytes 1179656 | tf_op jit(solution)/shard_map/while/body/eval_jaxpr/ppermute | solution.py:14
  505.3 36.4 %collective-permute-start.2 = (f32[1,16,16,384]{3,2,1,0:T(8,128)S(1)}, f32[1,16,16,384]{3,2,1,0:T(8,128)S(1)}, u32[]{:S(2)}, u32[]{:S(2)}) collective-permute-start(f32[1,16,16,384]{3,2,1,0:T(8,128)S(1)} %get-tuple-element.1500), channel_id=1, source_target_pairs={{0,8},{8,16},{16,24},{1,9},{9,17},{17,25},{2,10},{10,18},{18,26},{... | collective-permute-start | bytes 1179656 | tf_op jit(solution)/shard_map/while/body/eval_jaxpr/ppermute | solution.py:14
  545.6 11.2 %collective-permute-start.3 = (f32[1,16,16,384]{3,2,1,0:T(8,128)}, f32[1,16,16,384]{3,2,1,0:T(8,128)S(1)}, u32[]{:S(2)}, u32[]{:S(2)}) collective-permute-start(f32[1,16,16,384]{3,2,1,0:T(8,128)} %get-tuple-element.1515), channel_id=1, source_target_pairs={{8,0},{16,8},{24,16},{9,1},{17,9},{25,17},{10,2},{18,10},{26,18},{... | collective-permute-start | bytes 1179656 | tf_op jit(solution)/shard_map/while/body/eval_jaxpr/ppermute | solution.py:14
  557.6 32.8 %collective-permute-start.3 = (f32[1,16,16,384]{3,2,1,0:T(8,128)}, f32[1,16,16,384]{3,2,1,0:T(8,128)S(1)}, u32[]{:S(2)}, u32[]{:S(2)}) collective-permute-start(f32[1,16,16,384]{3,2,1,0:T(8,128)} %get-tuple-element.1515), channel_id=1, source_target_pairs={{8,0},{16,8},{24,16},{9,1},{17,9},{25,17},{10,2},{18,10},{26,18},{... | collective-permute-start | bytes 1179656 | tf_op jit(solution)/shard_map/while/body/eval_jaxpr/ppermute | solution.py:14
  591.1 75.3 %collective-permute-start.3 = (f32[1,16,16,384]{3,2,1,0:T(8,128)}, f32[1,16,16,384]{3,2,1,0:T(8,128)S(1)}, u32[]{:S(2)}, u32[]{:S(2)}) collective-permute-start(f32[1,16,16,384]{3,2,1,0:T(8,128)} %get-tuple-element.1515), channel_id=1, source_target_pairs={{8,0},{16,8},{24,16},{9,1},{17,9},{25,17},{10,2},{18,10},{26,18},{... | collective-permute-start | bytes 1179656 | tf_op jit(solution)/shard_map/while/body/eval_jaxpr/ppermute | solution.py:14
  689.1 10.8 %collective-permute-start.3 = (f32[1,16,16,384]{3,2,1,0:T(8,128)}, f32[1,16,16,384]{3,2,1,0:T(8,128)S(1)}, u32[]{:S(2)}, u32[]{:S(2)}) collective-permute-start(f32[1,16,16,384]{3,2,1,0:T(8,128)} %get-tuple-element.1515), channel_id=1, source_target_pairs={{8,0},{16,8},{24,16},{9,1},{17,9},{25,17},{10,2},{18,10},{26,18},{... | collective-permute-start | bytes 1179656 | tf_op jit(solution)/shard_map/while/body/eval_jaxpr/ppermute | solution.py:14
  722.5 10.8 %collective-permute-start.3 = (f32[1,16,16,384]{3,2,1,0:T(8,128)}, f32[1,16,16,384]{3,2,1,0:T(8,128)S(1)}, u32[]{:S(2)}, u32[]{:S(2)}) collective-permute-start(f32[1,16,16,384]{3,2,1,0:T(8,128)} %get-tuple-element.1515), channel_id=1, source_target_pairs={{8,0},{16,8},{24,16},{9,1},{17,9},{25,17},{10,2},{18,10},{26,18},{... | collective-permute-start | bytes 1179656 | tf_op jit(solution)/shard_map/while/body/eval_jaxpr/ppermute | solution.py:14
  755.9 10.8 %collective-permute-start.3 = (f32[1,16,16,384]{3,2,1,0:T(8,128)}, f32[1,16,16,384]{3,2,1,0:T(8,128)S(1)}, u32[]{:S(2)}, u32[]{:S(2)}) collective-permute-start(f32[1,16,16,384]{3,2,1,0:T(8,128)} %get-tuple-element.1515), channel_id=1, source_target_pairs={{8,0},{16,8},{24,16},{9,1},{17,9},{25,17},{10,2},{18,10},{26,18},{... | collective-permute-start | bytes 1179656 | tf_op jit(solution)/shard_map/while/body/eval_jaxpr/ppermute | solution.py:14
  799.3 170.1 %reduce-scatter.5.cloned.1.call-start = ((), (), s32[]{:S(2)}) async-start(), calls=%async_computation.3 | async-start | bytes 11943936 | tf_op jit(solution)/shard_map/reduce_scatter | solution.py:235
  (49 other events, 183.1 us)
Sparse Core Ops, SparseCore 0:
  799.4 58.0 reduce-scatter.2
  860.4 108.9 reduce-scatter.4
where the time goes:
time: 980 us; the launch traced here: 976 us
  waiting for transfers between devices  451 us (46%)
  other arithmetic  152 us (16%)
  starting transfers between devices  145 us (15%)
  local copies, waits for them, and re-layouts  105 us (11%)
  matrix products  94.4 us (10%)
  loops' own time  14.5 us (1%)
  between operations  14.1 us (1%)
    ppermute x28, waiting for transfers between devices, passed_along(): lax.ppermute(value, axis, [(source, source + steps) for source in range(i...  281 us
    ppermute x28, starting transfers between devices, passed_along(): lax.ppermute(value, axis, [(source, source + steps) for source in range(i...  145 us
    reduce_scatter x1, waiting for transfers between devices, shards(): lax.psum_scatter(dec_acc[None], 'dp', scatter_dimension=3, tiled=True)  112 us
    dynamic_update_slice x35, other arithmetic, store_row(): lax.dynamic_update_slice_in_dim(buffer, jnp.where(active, piece, kept), s...  67.8 us
    reduce_scatter x1, waiting for transfers between devices, shards(): lax.psum_scatter(enc_acc[None], 'dp', scatter_dimension=3, tiled=True)  57.5 us
    cond x80, local copies, waits for them, and re-layouts  44.1 us
    dot_general x72, matrix products, conv_back(): lax.dot_general(window, weight[row_off, col_off], (((1,), (1,)), ((), ())...  41.7 us
    dot_general x72, matrix products, conv_apply(): jnp.dot(window, weight[row_off, col_off], preferred_element_type=jnp.floa...  28.1 us
  transfers between devices with their start and end apart: 30, of which 30 were waited for; matrix products, arithmetic and copies ran while one was open for 4% of the time, Pallas kernels for 0%

commit v1 on v0

v1 whole, which is shorter than its diff:
```python
import functools
import math

import jax
import jax.numpy as jnp
from jax import lax
from jax.experimental import pallas as pl
from jax.experimental.pallas import tpu as pltpu
from jax.sharding import PartitionSpec as P

GROUPS = 32
F32 = jnp.float32
BF16 = jnp.bfloat16
ENC_FWD, DEC_FWD, DEC_BWD, ENC_BWD = 1, 2, 3, 4
VMEM_LIMIT = 40 * 1024 * 1024


def embed(stamps_in, channels):
    half_width = channels // 2
    frequency = jnp.exp(-math.log(10000.0) * jnp.arange(half_width, dtype=jnp.float32) / half_width)
    angles = stamps_in.astype(jnp.float32)[:, None] * frequency[None, :]
    return jnp.concatenate([jnp.sin(angles), jnp.cos(angles)], axis=1)


def noise_levels(stamps_in):
    phase = (stamps_in.astype(jnp.float32) / 1000.0 + 0.008) / 1.008 * (math.pi / 2.0)
    signal = jnp.cos(phase) ** 2
    return (jnp.sqrt(signal), jnp.sqrt(1.0 - signal))


def stage_of(position, sections):
    lap, step = divmod(position, sections)
    section = step if lap % 2 == 0 else sections - 1 - step
    return section, lap + 1


def make_schedule(sections, samples):
    stages = 4 * sections
    ticks = []
    for tick in range(stages + 2 * (samples - 1)):
        work, moves = {}, []
        for sample in range(samples):
            position = tick - 2 * sample
            if not 0 <= position < stages:
                continue
            section, op = stage_of(position, sections)
            assert section not in work
            work[section] = (op, sample)
            if position + 1 < stages:
                target, _ = stage_of(position + 1, sections)
                if target != section:
                    moves.append((section, target))
        ticks.append((work, moves))
    return ticks


def schedule_table(ticks, sections):
    table = []
    for section in range(sections):
        row = []
        for work, _ in ticks:
            op, sample = work.get(section, (0, 0))
            first, last = section == 0, section == sections - 1
            from_here = (
                (op == ENC_FWD and first)
                or (op == DEC_FWD and last)
                or (op == DEC_BWD and first)
                or (op == ENC_BWD and last)
            )
            to_here = (
                op == ENC_FWD or (op == DEC_FWD and first) or (op == DEC_BWD and last)
            )
            row += [op, sample, int(from_here), int(to_here)]
        table.append(row)
    return table


def group_sums(vectors, members):
    channels = vectors[0].shape[1]
    row = lax.broadcasted_iota(jnp.int32, (16, channels), 0)
    stacked = jnp.zeros((16, channels), F32)
    for index, vector in enumerate(vectors):
        high = vector.astype(BF16).astype(F32)
        rest = vector - high
        middle = rest.astype(BF16).astype(F32)
        for part_index, part in enumerate((high, middle, rest - middle)):
            stacked = jnp.where(row == 3 * index + part_index, part, stacked)
    summed = jnp.dot(stacked.astype(BF16), members, preferred_element_type=F32)
    return [
        summed[3 * i : 3 * i + 1] + summed[3 * i + 1 : 3 * i + 2] + summed[3 * i + 2 : 3 * i + 3]
        for i in range(len(vectors))
    ]


def spread_columns(field, breadth, windows_ref):
    pixels, channels = field.shape
    column = lax.broadcasted_iota(jnp.int32, (pixels, channels), 0) & (breadth - 1)
    before = jnp.where(column == 0, 0.0, pltpu.roll(field, 1, 0))
    after = jnp.where(column == breadth - 1, 0.0, pltpu.roll(field, pixels - 1, 0))
    edge = jnp.zeros((breadth, channels), BF16)
    for index, shifted in enumerate((before, field, after)):
        lanes = slice(index * channels, (index + 1) * channels)
        windows_ref[0:breadth, lanes] = edge
        windows_ref[breadth : breadth + pixels, lanes] = shifted.astype(BF16)
        windows_ref[breadth + pixels : 2 * breadth + pixels, lanes] = edge


def convolve(windows_ref, weight_ref, pixels, breadth):
    taps, channels, outputs = weight_ref.shape
    total = None
    for row in range(3):
        part = jnp.dot(
            windows_ref[row * breadth : row * breadth + pixels, :],
            weight_ref[3 * row : 3 * row + 3].reshape(3 * channels, outputs),
            preferred_element_type=F32,
        )
        total = part if total is None else total + part
    return total


def convolve_back(windows_ref, weight_ref, pixels, breadth):
    taps, channels, outputs = weight_ref.shape
    total = None
    for row in range(3):
        for col in range(3):
            part = lax.dot_general(
                windows_ref[
                    (2 - row) * breadth : (2 - row) * breadth + pixels,
                    (2 - col) * outputs : (3 - col) * outputs,
                ],
                weight_ref[3 * row + col],
                (((1,), (1,)), ((), ())),
                preferred_element_type=F32,
            )
            total = part if total is None else total + part
    return total


def stage_kernel(
    tick,
    aside,
    sections,
    breadth,
    factor,
    has_forward,
    has_backward,
    table,
    arriving,
    modulation,
    members,
    enc_weight,
    dec_weight,
    noise,
    _kept,
    _side,
    _normed,
    _scale,
    _acts,
    _cots,
    leaving,
    kept,
    side,
    normed,
    scale,
    acts,
    cots,
    x_buf,
    e_buf,
    n_buf,
    h_buf,
    r_buf,
    a_buf,
    y_buf,
    m_buf,
    w_buf,
    windows,
    sems,
):
    pixels, channels = x_buf.shape
    op = table[4 * tick]
    slot = table[4 * tick + 1]
    from_here = table[4 * tick + 2]
    to_here = table[4 * tick + 3]
    is_enc = jnp.logical_or(op == ENC_FWD, op == ENC_BWD)

    def copy(source, target, sem):
        return pltpu.make_async_copy(source, target, sems.at[sem])

    group_size = channels // GROUPS
    if aside:
        kind = 2
        inverse_count = 1.0 / (pixels * 2 * group_size)
    else:
        kind = jnp.where(is_enc, 0, 1)
        inverse_count = jnp.where(
            is_enc, 1.0 / (pixels * group_size), 1.0 / (pixels * 2 * group_size)
        ).astype(F32)

    def start_weight():
        if aside:
            copy(dec_weight.at[:, channels : 2 * channels, :], w_buf, 0).start()
            copy(members.at[1], m_buf, 1).start()
        else:

            @pl.when(is_enc)
            def _():
                copy(enc_weight, w_buf, 0).start()

            @pl.when(jnp.logical_not(is_enc))
            def _():
                copy(dec_weight.at[:, 0:channels, :], w_buf, 0).start()

            copy(members.at[kind], m_buf, 1).start()

    def start_input():
        if aside:
            copy(kept.at[slot], x_buf, 2).start()
        else:

            @pl.when(from_here == 1)
            def _():
                copy(kept.at[slot], x_buf, 2).start()

            @pl.when(from_here == 0)
            def _():
                copy(arriving, x_buf, 2).start()

    def forward():
        start_input()
        start_weight()
        is_dec = op == DEC_FWD
        if not aside:

            @pl.when(is_dec)
            def _():
                copy(side.at[slot], e_buf, 3).start()

                @pl.when(to_here == 1)
                def _():
                    copy(noise.at[slot], n_buf, 4).start()

        copy(kept.at[slot], x_buf, 2).wait()
        copy(members.at[0], m_buf, 1).wait()
        x = x_buf[...]
        total = jnp.sum(x, axis=0, keepdims=True)
        own_mean = total * (1.0 / pixels)
        own_dev = x - own_mean
        own_square = jnp.sum(own_dev * own_dev, axis=0, keepdims=True)
        (group_total,) = group_sums([total], m_buf[...])
        mean = group_total * inverse_count
        apart = own_mean - mean
        (group_square,) = group_sums([own_square + pixels * (apart * apart)], m_buf[...])
        inverse_std = lax.rsqrt(group_square * inverse_count + 1e-05)
        unit = (x - mean) * inverse_std
        value = unit * modulation[kind, slot]
        active = value / (1.0 + jnp.exp(-value))
        h_buf[...] = unit
        r_buf[...] = inverse_std
        a_buf[...] = active.astype(BF16)
        spread_columns(active, breadth, windows)
        copy(h_buf, normed.at[kind, slot], 5).start()
        copy(r_buf, scale.at[kind, slot], 6).start()
        copy(a_buf, acts.at[kind, slot], 7).start()
        copy(enc_weight, w_buf, 0).wait()
        y = convolve(windows, w_buf, pixels, breadth)
        if aside:
            y_buf[...] = y
            out = copy(y_buf, side.at[slot], 8)
            out.start()
            out.wait()
        else:
            y = y + x_buf[...]
            y_buf[...] = y

            @pl.when(is_dec)
            def _():
                copy(side.at[slot], e_buf, 3).wait()
                y_buf[...] = y_buf[...] + e_buf[...]

                @pl.when(to_here == 1)
                def _():
                    copy(noise.at[slot], n_buf, 4).wait()
                    y_buf[...] = factor * (y_buf[...] - n_buf[...].astype(F32))

            send_result()
        copy(h_buf, normed.at[kind, slot], 5).wait()
        copy(r_buf, scale.at[kind, slot], 6).wait()
        copy(a_buf, acts.at[kind, slot], 7).wait()

    def send_result():
        out = copy(y_buf, leaving, 8)
        out.start()

        @pl.when(to_here == 1)
        def _():
            stay = copy(y_buf, kept.at[slot], 9)
            stay.start()
            stay.wait()

        out.wait()

    def backward():
        start_weight()
        which = 1 if aside else 1 - jnp.where(is_enc, 1, 0)
        if aside:
            copy(cots.at[1, slot], a_buf, 7).start()
        else:
            start_input()

            @pl.when(is_enc)
            def _():
                copy(side.at[slot], e_buf, 3).start()

        copy(normed.at[kind, slot], h_buf, 5).start()
        copy(scale.at[kind, slot], r_buf, 6).start()
        if aside:
            copy(cots.at[1, slot], a_buf, 7).wait()
            spread_columns(a_buf[...].astype(F32), breadth, windows)
        else:
            copy(kept.at[slot], x_buf, 2).wait()

            @pl.when(is_enc)
            def _():
                copy(side.at[slot], e_buf, 3).wait()
                x_buf[...] = x_buf[...] + e_buf[...]

            g = x_buf[...]
            a_buf[...] = g.astype(BF16)
            copy(a_buf, cots.at[which, slot], 7).start()
            spread_columns(g, breadth, windows)
        copy(enc_weight, w_buf, 0).wait()
        down = convolve_back(windows, w_buf, pixels, breadth)
        copy(normed.at[kind, slot], h_buf, 5).wait()
        copy(scale.at[kind, slot], r_buf, 6).wait()
        copy(members.at[0], m_buf, 1).wait()
        unit = h_buf[...]
        mod = modulation[kind, slot]
        value = unit * mod
        gate = 1.0 / (1.0 + jnp.exp(-value))
        slope = gate * (1.0 + value * (1.0 - gate))
        d_unit = down * slope * mod
        sums = group_sums(
            [
                jnp.sum(d_unit, axis=0, keepdims=True),
                jnp.sum(d_unit * unit, axis=0, keepdims=True),
            ],
            m_buf[...],
        )
        shift, stretch = sums[0] * inverse_count, sums[1] * inverse_count
        result = r_buf[...] * (d_unit - shift - unit * stretch)
        if aside:
            y_buf[...] = result
            out = copy(y_buf, side.at[slot], 8)
            out.start()
            out.wait()
        else:
            y_buf[...] = result + x_buf[...]
            send_result()
            copy(a_buf, cots.at[which, slot], 7).wait()

    if has_forward:
        pl.when(op == ENC_FWD if aside else jnp.logical_or(op == ENC_FWD, op == DEC_FWD))(forward)
    if has_backward:
        pl.when(op == DEC_BWD if aside else op >= DEC_BWD)(backward)


def call_stage(tick, aside, sections, breadth, factor, ops, table, arriving, consts, state):
    samples, pixels, channels = state[0].shape
    any_spec = pl.BlockSpec(memory_space=pl.ANY)
    vmem = pl.BlockSpec(memory_space=pltpu.VMEM)
    smem = pl.BlockSpec(memory_space=pltpu.SMEM)
    block = jax.ShapeDtypeStruct((pixels, channels), F32)
    n_state = len(state)
    fresh = state[1] is None or not isinstance(state[1], jax.Array)
    if aside:
        has_forward, has_backward = ENC_FWD in ops, DEC_BWD in ops
    else:
        has_forward = ENC_FWD in ops or DEC_FWD in ops
        has_backward = DEC_BWD in ops or ENC_BWD in ops
    modulation, members, enc_weight, dec_weight, noise = consts
    body = functools.partial(
        stage_kernel, tick, aside, sections, breadth, factor, has_forward, has_backward
    )
    given = [table, arriving, modulation, members, enc_weight, dec_weight, noise]
    first_state = len(given)
    present = [i for i, leaf in enumerate(state) if not isinstance(leaf, jax.ShapeDtypeStruct)]

    def kernel(*refs):
        head = list(refs[:first_state])
        tail = list(refs[first_state + len(present) :])
        if aside:
            tail = [None] + tail
        body(*head, *([None] * n_state), *tail)

    state_shapes = [jax.ShapeDtypeStruct(leaf.shape, leaf.dtype) for leaf in state]
    shift = 0 if aside else 1
    outs = pl.pallas_call(
        kernel,
        out_shape=([] if aside else [block]) + state_shapes,
        in_specs=[smem, any_spec, vmem] + [any_spec] * (4 + len(present)),
        out_specs=[any_spec] * (n_state + shift),
        scratch_shapes=[
            pltpu.VMEM((pixels, channels), F32),
            pltpu.VMEM((pixels, channels), F32),
            pltpu.VMEM((pixels, channels), BF16),
            pltpu.VMEM((pixels, channels), F32),
            pltpu.VMEM((1, channels), F32),
            pltpu.VMEM((pixels, channels), BF16),
            pltpu.VMEM((pixels, channels), F32),
            pltpu.VMEM((channels, channels), BF16),
            pltpu.VMEM(enc_weight.shape, BF16),
            pltpu.VMEM((pixels + 2 * breadth, 3 * channels), BF16),
            pltpu.SemaphoreType.DMA((10,)),
        ],
        input_output_aliases={first_state + j: i + shift for j, i in enumerate(present)},
        compiler_params=pltpu.CompilerParams(vmem_limit_bytes=VMEM_LIMIT),
        cost_estimate=pl.CostEstimate(
            flops=2 * 9 * pixels * channels * channels,
            bytes_accessed=10 * pixels * channels * 4,
            transcendentals=0,
        ),
    )(*given, *[state[i] for i in present])
    outs = list(outs)
    if aside:
        return None, outs
    return outs[0], outs[1:]


def weight_grad_kernel(breadth, acts, cots, out, flipped, windows):
    halves, samples, pixels, channels = acts.shape
    tap = pl.program_id(0)

    @pl.when(tap == 0)
    def _():
        for half in range(halves):
            for sample in range(samples):
                flipped[
                    half * channels : (half + 1) * channels, sample * pixels : (sample + 1) * pixels
                ] = acts[half, sample].astype(F32).T.astype(BF16)
        edge = jnp.zeros((breadth, channels), BF16)
        column = lax.broadcasted_iota(jnp.int32, (pixels, channels), 0) & (breadth - 1)
        for sample in range(samples):
            field = cots[0, sample].astype(F32)
            before = jnp.where(column == 0, 0.0, pltpu.roll(field, 1, 0))
            after = jnp.where(column == breadth - 1, 0.0, pltpu.roll(field, pixels - 1, 0))
            for index, shifted in enumerate((before, field, after)):
                windows[index, sample, 0:breadth, :] = edge
                windows[index, sample, breadth : breadth + pixels, :] = shifted.astype(BF16)
                windows[index, sample, breadth + pixels : 2 * breadth + pixels, :] = edge

    row, col = tap // 3, tap % 3
    start = pl.multiple_of((2 - row) * breadth, breadth)
    total = None
    for sample in range(samples):
        part = jnp.dot(
            flipped[:, sample * pixels : (sample + 1) * pixels],
            windows[2 - col, sample, pl.ds(start, pixels), :],
            preferred_element_type=F32,
        )
        total = part if total is None else total + part
    out[0] = total


def weight_grad(acts, cots, halves, breadth):
    _, samples, pixels, channels = acts.shape
    first_half = 0 if halves == 1 else 1
    which = 0 if halves == 1 else 1
    acts = acts[first_half : first_half + halves]
    return pl.pallas_call(
        functools.partial(weight_grad_kernel, breadth),
        grid=(9,),
        out_shape=jax.ShapeDtypeStruct((9, halves * channels, channels), F32),
        in_specs=[
            pl.BlockSpec((halves, samples, pixels, channels), lambda tap: (0, 0, 0, 0)),
            pl.BlockSpec((1, samples, pixels, channels), lambda tap: (which, 0, 0, 0)),
        ],
        out_specs=pl.BlockSpec((1, halves * channels, channels), lambda tap: (tap, 0, 0)),
        scratch_shapes=[
            pltpu.VMEM((halves * channels, samples * pixels), BF16),
            pltpu.VMEM((3, samples, pixels + 2 * breadth, channels), BF16),
        ],
        compiler_params=pltpu.CompilerParams(vmem_limit_bytes=VMEM_LIMIT),
        cost_estimate=pl.CostEstimate(
            flops=2 * 9 * samples * pixels * channels * channels * halves,
            bytes_accessed=9 * halves * channels * channels * 4,
            transcendentals=0,
        ),
    )(acts, cots)


def shards(clean, noise, stamps, enc_weight, dec_weight):
    sections = lax.axis_size("section")
    section_index = lax.axis_index("section")
    samples, height, breadth, channels = clean.shape
    pixels = height * breadth
    factor = 1.0 / math.sqrt(samples * lax.axis_size("dp") * pixels)

    ticks = make_schedule(sections, samples)
    table = jnp.asarray(schedule_table(ticks, sections), jnp.int32)[section_index]

    keep_level, spread_level = noise_levels(stamps)
    noise = noise.reshape(samples, pixels, channels)
    noisy = keep_level[:, None, None] * clean.reshape(noise.shape).astype(F32) + spread_level[
        :, None, None
    ] * noise.astype(F32)

    wide = embed(stamps, 2 * channels)
    modulation = 1.0 + 0.5 * jnp.stack(
        [embed(stamps, channels), wide[:, :channels], wide[:, channels:]]
    )
    modulation = modulation[:, :, None, :]
    channel = jnp.arange(channels)
    group_size = channels // GROUPS
    members = jnp.stack(
        [
            (channel[:, None] // size == channel[None, :] // size).astype(BF16)
            for size in (group_size, 2 * group_size)
        ]
    )
    enc_kernel = enc_weight.reshape(9, channels, channels)
    dec_kernel = dec_weight.reshape(9, 2 * channels, channels)
    consts = (modulation, members, enc_kernel, dec_kernel, noise)

    fresh = jax.ShapeDtypeStruct
    state = [
        noisy,
        fresh((samples, pixels, channels), F32),
        fresh((3, samples, pixels, channels), F32),
        fresh((3, samples, 1, channels), F32),
        fresh((3, samples, pixels, channels), BF16),
        fresh((2, samples, pixels, channels), BF16),
    ]
    arriving = noisy[0]
    dec_done = max(
        tick for tick, (work, _) in enumerate(ticks) if any(w[0] == DEC_BWD for w in work.values())
    )
    dec_share = None
    for tick, (work, moves) in enumerate(ticks):
        ops = {op for op, _ in work.values()}
        leaving, state = call_stage(
            tick, False, sections, breadth, factor, ops, table, arriving, consts, state
        )
        if moves:
            arriving = lax.ppermute(leaving, "section", moves)
        if ops & {ENC_FWD, DEC_BWD}:
            _, state = call_stage(
                tick, True, sections, breadth, factor, ops, table, arriving_before(leaving), consts, state
            )
        if tick == dec_done:
            dec_grad = weight_grad(state[4], state[5], 2, breadth)
            dec_share = lax.psum_scatter(
                dec_grad.reshape((1, 3, 3, 2 * channels, channels)),
                "dp",
                scatter_dimension=3,
                tiled=True,
            )
    enc_grad = weight_grad(state[4], state[5], 1, breadth)
    enc_share = lax.psum_scatter(
        enc_grad.reshape((1, 3, 3, channels, channels)), "dp", scatter_dimension=3, tiled=True
    )
    return (enc_share, dec_share)


def arriving_before(leaving):
    return leaving


def solution(mesh):
    placed = (
        P("dp", None, None, None),
        P("dp", None, None, None),
        P("dp"),
        P("section", None, None, None, None),
        P("section", None, None, None, None),
    )
    return jax.shard_map(
        shards,
        mesh=mesh,
        in_specs=placed,
        out_specs=(P("section", None, None, "dp", None), P("section", None, None, "dp", None)),
        check_vma=False,
    )
```

time: 980 us -> 523 us (0.53)
  waiting for transfers between devices: 451 us -> 249 us
  other arithmetic: 152 us -> 4.06 us
  Pallas kernels: 0 us -> 126 us
  matrix products: 94.4 us -> 0 us
  local copies, waits for them, and re-layouts: 105 us -> 15.2 us
  starting transfers between devices: 145 us -> 104 us
  loops' own time: 14.5 us -> 0 us
    ppermute x28 -> x21, waiting for transfers between devices: 281 us -> 76.5 us  [shards(): arriving = lax.ppermute(leaving, 'section', moves)]
    pallas_call x0 -> x42, Pallas kernels: none -> 126 us  [the longest x40 110 us: call_stage(): pl.pallas_call(kernel, out_shape=([] if aside else [block]) + state_shape...]
    dot_general x216 -> x0, matrix products: 94.4 us -> none  [the longest x72 41.7 us: conv_back(): lax.dot_general(window, weight[row_off, col_off], (((1,), (1,)), ((), ())...]
    dynamic_update_slice x35 -> x0, other arithmetic: 67.8 us -> none  [store_row(): lax.dynamic_update_slice_in_dim(buffer, jnp.where(active, piece, kept), s...]
    cond x80 -> x0, local copies, waits for them, and re-layouts: 44.1 us -> none
    ppermute x28 -> x21, starting transfers between devices: 145 us -> 104 us  [shards(): arriving = lax.ppermute(leaving, 'section', moves)]
    dynamic_slice x30 -> x0, local copies, waits for them, and re-layouts: 24.2 us -> none  [pick_row(): return lax.dynamic_slice_in_dim(buffer, slot_index, 1, 0)]
    broadcast_in_dim x59 -> x0, local copies, waits for them, and re-layouts: 24 us -> none  [the longest x6 7.8 us: shards(): blank_buffer = jnp.zeros(clean.shape, jnp.float32)]
  transfers between devices with their start and end apart: 30 -> 23, of which waited for: 30 -> 13; matrix products, arithmetic and copies ran while one was open for 4% -> 0% of each run, Pallas kernels for 0% -> 10%
where the time goes in v1:
time: 523 us; the launch traced here: 514 us
  waiting for transfers between devices  249 us (48%)
  Pallas kernels  126 us (24%)
  starting transfers between devices  104 us (20%)
  local copies, waits for them, and re-layouts  15.2 us (3%)
  between operations  15.2 us (3%)
    reduce_scatter x1, waiting for transfers between devices, shards(): lax.psum_scatter(dec_grad.reshape((1, 3, 3, 2 * channels, channels)), 'dp...  112 us
    pallas_call x40, Pallas kernels, call_stage(): pl.pallas_call(kernel, out_shape=([] if aside else [block]) + state_shape...  110 us
    ppermute x21, starting transfers between devices, shards(): arriving = lax.ppermute(leaving, 'section', moves)  104 us
    ppermute x21, waiting for transfers between devices, shards(): arriving = lax.ppermute(leaving, 'section', moves)  76.5 us
    reduce_scatter x1, waiting for transfers between devices, shards(): lax.psum_scatter(enc_grad.reshape((1, 3, 3, channels, channels)), 'dp', s...  60.2 us
    pallas_call x2, Pallas kernels, weight_grad(): pl.pallas_call(functools.partial(weight_grad_kernel, breadth), grid=(9,),...  16.7 us
    unnamed x22, local copies, waits for them, and re-layouts  13.4 us
  transfers between devices with their start and end apart: 23, of which 13 were waited for; matrix products, arithmetic and copies ran while one was open for 0% of the time, Pallas kernels for 10%

profile of v1, /device:TPU:0, one launch (start us, length us, event | category | flops | bytes accessed | tf_op | source)
XLA Modules:
  0.0 513.8 jit_solution(5706630613397550774)
XLA Ops:
  37.3 12.4 %collective-permute-start.2 = (f32[256,384]{1,0:T(8,128)S(1)}, f32[256,384]{1,0:T(8,128)S(1)}, u32[]{:S(2)}, u32[]{:S(2)}) collective-permute-start(f32[256,384]{1,0:T(8,128)S(1)} %get-tuple-element.285.refs_1_), channel_id=1, source_target_pairs={{16,24},{0,8},{17,25},{1,9},{18,26},{2,10},{19,27},{3,11},{20,28},... | collective-permute-start | bytes 1179656 | tf_op jit(solution)/shard_map/ppermute | solution.py:544
  62.4 12.0 %collective-permute-start.4 = (f32[256,384]{1,0:T(8,128)S(1)}, f32[256,384]{1,0:T(8,128)S(1)}, u32[]{:S(2)}, u32[]{:S(2)}) collective-permute-start(f32[256,384]{1,0:T(8,128)S(1)} %get-tuple-element.311.refs_1_), channel_id=1, source_target_pairs={{24,16},{16,24},{0,8},{25,17},{17,25},{1,9},{26,18},{18,26},{2,10}... | collective-permute-start | bytes 1179656 | tf_op jit(solution)/shard_map/ppermute | solution.py:544
  86.1 18.8 %collective-permute-start.6 = (f32[256,384]{1,0:T(8,128)S(1)}, f32[256,384]{1,0:T(8,128)S(1)}, u32[]{:S(2)}, u32[]{:S(2)}) collective-permute-start(f32[256,384]{1,0:T(8,128)S(1)} %get-tuple-element.337.refs_1_), channel_id=1, source_target_pairs={{8,0},{24,16},{16,24},{0,8},{9,1},{25,17},{17,25},{1,9},{10,2},{26... | collective-permute-start | bytes 1179656 | tf_op jit(solution)/shard_map/ppermute | solution.py:544
  116.2 4.5 shard_map.93
  120.7 11.7 %collective-permute-start.8 = (f32[256,384]{1,0:T(8,128)S(1)}, f32[256,384]{1,0:T(8,128)S(1)}, u32[]{:S(2)}, u32[]{:S(2)}) collective-permute-start(f32[256,384]{1,0:T(8,128)S(1)} %get-tuple-element.363.refs_1_), channel_id=1, source_target_pairs={{0,8},{8,0},{24,16},{16,24},{1,9},{9,1},{25,17},{17,25},{2,10},{10... | collective-permute-start | bytes 1179656 | tf_op jit(solution)/shard_map/ppermute | solution.py:544
  132.4 4.3 shard_map.94
  143.8 4.8 shard_map.97
  148.5 14.6 %collective-permute-start.10 = (f32[256,384]{1,0:T(8,128)S(1)}, f32[256,384]{1,0:T(8,128)S(1)}, u32[]{:S(2)}, u32[]{:S(2)}) collective-permute-start(f32[256,384]{1,0:T(8,128)S(1)} %get-tuple-element.389.refs_1_), channel_id=1, source_target_pairs={{16,24},{0,8},{8,0},{24,16},{17,25},{1,9},{9,1},{25,17},{18,26},{2... | collective-permute-start | bytes 1179656 | tf_op jit(solution)/shard_map/ppermute | solution.py:544
  167.4 4.7 collective-permute-done.10.refs_1_
  177.7 4.5 shard_map.101
  182.2 12.4 %collective-permute-start.12 = (f32[256,384]{1,0:T(8,128)S(1)}, f32[256,384]{1,0:T(8,128)S(1)}, u32[]{:S(2)}, u32[]{:S(2)}) collective-permute-start(f32[256,384]{1,0:T(8,128)S(1)} %get-tuple-element.415.refs_1_), channel_id=1, source_target_pairs={{24,16},{16,24},{0,8},{8,0},{25,17},{17,25},{1,9},{9,1},{26,18},{1... | collective-permute-start | bytes 1179656 | tf_op jit(solution)/shard_map/ppermute | solution.py:544
  198.9 4.4 collective-permute-done.12.refs_1_
  208.9 4.4 shard_map.105
  213.2 9.0 %collective-permute-start.14 = (f32[256,384]{1,0:T(8,128)S(1)}, f32[256,384]{1,0:T(8,128)S(1)}, u32[]{:S(2)}, u32[]{:S(2)}) collective-permute-start(f32[256,384]{1,0:T(8,128)S(1)} %get-tuple-element.441.refs_1_), channel_id=1, source_target_pairs={{8,0},{24,16},{16,24},{0,8},{9,1},{25,17},{17,25},{1,9},{10,2},{26... | collective-permute-start | bytes 1179656 | tf_op jit(solution)/shard_map/ppermute | solution.py:544
  222.3 4.3 shard_map.106
  226.6 4.4 collective-permute-done.14.refs_1_
  238.9 19.8 %collective-permute-done.16.refs_1_ = f32[256,384]{1,0:T(8,128)S(1)} collective-permute-done((f32[256,384]{1,0:T(8,128)S(1)}, f32[256,384]{1,0:T(8,128)S(1)}, u32[]{:S(2)}, u32[]{:S(2)}) %collective-permute-start.16) | collective-permute-done | bytes 393248 | tf_op jit(solution)/shard_map/ppermute | solution.py:544
  265.0 10.3 %shard_map.118 = f32[9,768,384]{2,1,0:T(8,128)S(1)} custom-call(bf16[2,4,256,384]{3,2,1,0:T(8,128)(2,1)S(1)} %slice.11.acts, bf16[2,4,256,384]{3,2,1,0:T(8,128)(2,1)S(1)} %get-tuple-element.492.refs_12_.cots), custom_call_target="tpu_custom_call" | custom-call | flops 5435817984 | bytes 10616832 | tf_op jit(solution)/shard_map/pallas_call | solution.py:469
  281.5 8.4 %collective-permute-done.18.refs_1_ = f32[256,384]{1,0:T(8,128)S(1)} collective-permute-done((f32[256,384]{1,0:T(8,128)S(1)}, f32[256,384]{1,0:T(8,128)S(1)}, u32[]{:S(2)}, u32[]{:S(2)}) %collective-permute-start.18) | collective-permute-done | bytes 393248 | tf_op jit(solution)/shard_map/ppermute | solution.py:544
  296.3 24.2 %collective-permute-done.20.refs_1_ = f32[256,384]{1,0:T(8,128)S(1)} collective-permute-done((f32[256,384]{1,0:T(8,128)S(1)}, f32[256,384]{1,0:T(8,128)S(1)}, u32[]{:S(2)}, u32[]{:S(2)}) %collective-permute-start.20) | collective-permute-done | bytes 393248 | tf_op jit(solution)/shard_map/ppermute | solution.py:544
  320.5 4.3 shard_map.116
  324.9 6.4 %shard_map.117 = f32[9,384,384]{2,1,0:T(8,128)S(1)} custom-call(bf16[1,4,256,384]{3,2,1,0:T(8,128)(2,1)S(1)} %slice.10.acts, bf16[2,4,256,384]{3,2,1,0:T(8,128)(2,1)S(1)} %get-tuple-element.515.cots), custom_call_target="tpu_custom_call" | custom-call | flops 2717908992 | bytes 5308416 | tf_op jit(solution)/shard_map/pallas_call | solution.py:469
  334.4 60.2 %reduce-scatter.3.cloned.1.call-done = f32[1,3,3,48,384]{4,3,2,1,0:T(8,128)} async-done(((f32[1,3,3,384,384]{4,3,2,1,0:T(8,128)}), f32[1,3,3,48,384]{4,3,2,1,0:T(8,128)}) %reduce-scatter.3.cloned.1.call-update) | async-done | bytes 663568 | tf_op jit(solution)/shard_map/reduce_scatter | solution.py:558
  394.6 111.9 %reduce-scatter.5.cloned.1.call-done = f32[1,3,3,96,384]{4,3,2,1,0:T(8,128)} async-done(((f32[1,3,3,768,384]{4,3,2,1,0:T(8,128)}), f32[1,3,3,96,384]{4,3,2,1,0:T(8,128)}) %reduce-scatter.5.cloned.1.call-update) | async-done | bytes 1327120 | tf_op jit(solution)/shard_map/reduce_scatter | solution.py:551
  (106 shorter events, 122.0 us)
Async XLA Ops:
  7.2 387.5 %reduce-scatter.3.cloned.1.call-start = ((), (), s32[]{:S(2)}) async-start(), calls=%async_computation.2 | async-start | bytes 5971968 | tf_op jit(solution)/shard_map/reduce_scatter | solution.py:558
  21.2 10.5 %collective-permute-start = (f32[256,384]{1,0:T(8,128)S(1)}, f32[256,384]{1,0:T(8,128)S(1)}, u32[]{:S(2)}, u32[]{:S(2)}) collective-permute-start(f32[256,384]{1,0:T(8,128)S(1)} %get-tuple-element.259.refs_1_), channel_id=1, source_target_pairs={{0,8},{1,9},{2,10},{3,11},{4,12},{5,13},{6,14},{7,15}} | collective-permute-start | bytes 1179656 | tf_op jit(solution)/shard_map/ppermute | solution.py:544
  32.3 1.4 collective-permute-start.1
  37.3 19.6 %collective-permute-start.2 = (f32[256,384]{1,0:T(8,128)S(1)}, f32[256,384]{1,0:T(8,128)S(1)}, u32[]{:S(2)}, u32[]{:S(2)}) collective-permute-start(f32[256,384]{1,0:T(8,128)S(1)} %get-tuple-element.285.refs_1_), channel_id=1, source_target_pairs={{16,24},{0,8},{17,25},{1,9},{18,26},{2,10},{19,27},{3,11},{20,28},... | collective-permute-start | bytes 1179656 | tf_op jit(solution)/shard_map/ppermute | solution.py:544
  57.5 1.4 collective-permute-start.3
  62.4 17.6 %collective-permute-start.4 = (f32[256,384]{1,0:T(8,128)S(1)}, f32[256,384]{1,0:T(8,128)S(1)}, u32[]{:S(2)}, u32[]{:S(2)}) collective-permute-start(f32[256,384]{1,0:T(8,128)S(1)} %get-tuple-element.311.refs_1_), channel_id=1, source_target_pairs={{24,16},{16,24},{0,8},{25,17},{17,25},{1,9},{26,18},{18,26},{2,10}... | collective-permute-start | bytes 1179656 | tf_op jit(solution)/shard_map/ppermute | solution.py:544
  80.7 1.8 collective-permute-start.5
  86.1 24.5 %collective-permute-start.6 = (f32[256,384]{1,0:T(8,128)S(1)}, f32[256,384]{1,0:T(8,128)S(1)}, u32[]{:S(2)}, u32[]{:S(2)}) collective-permute-start(f32[256,384]{1,0:T(8,128)S(1)} %get-tuple-element.337.refs_1_), channel_id=1, source_target_pairs={{8,0},{24,16},{16,24},{0,8},{9,1},{25,17},{17,25},{1,9},{10,2},{26... | collective-permute-start | bytes 1179656 | tf_op jit(solution)/shard_map/ppermute | solution.py:544
  114.8 1.4 collective-permute-start.7
  120.7 17.5 %collective-permute-start.8 = (f32[256,384]{1,0:T(8,128)S(1)}, f32[256,384]{1,0:T(8,128)S(1)}, u32[]{:S(2)}, u32[]{:S(2)}) collective-permute-start(f32[256,384]{1,0:T(8,128)S(1)} %get-tuple-element.363.refs_1_), channel_id=1, source_target_pairs={{0,8},{8,0},{24,16},{16,24},{1,9},{9,1},{25,17},{17,25},{2,10},{10... | collective-permute-start | bytes 1179656 | tf_op jit(solution)/shard_map/ppermute | solution.py:544
  142.4 1.4 collective-permute-start.9
  148.5 23.6 %collective-permute-start.10 = (f32[256,384]{1,0:T(8,128)S(1)}, f32[256,384]{1,0:T(8,128)S(1)}, u32[]{:S(2)}, u32[]{:S(2)}) collective-permute-start(f32[256,384]{1,0:T(8,128)S(1)} %get-tuple-element.389.refs_1_), channel_id=1, source_target_pairs={{16,24},{0,8},{8,0},{24,16},{17,25},{1,9},{9,1},{25,17},{18,26},{2... | collective-permute-start | bytes 1179656 | tf_op jit(solution)/shard_map/ppermute | solution.py:544
  176.3 1.4 collective-permute-start.11
  182.2 21.1 %collective-permute-start.12 = (f32[256,384]{1,0:T(8,128)S(1)}, f32[256,384]{1,0:T(8,128)S(1)}, u32[]{:S(2)}, u32[]{:S(2)}) collective-permute-start(f32[256,384]{1,0:T(8,128)S(1)} %get-tuple-element.415.refs_1_), channel_id=1, source_target_pairs={{24,16},{16,24},{0,8},{8,0},{25,17},{17,25},{1,9},{9,1},{26,18},{1... | collective-permute-start | bytes 1179656 | tf_op jit(solution)/shard_map/ppermute | solution.py:544
  207.5 1.4 collective-permute-start.13
  213.2 17.7 %collective-permute-start.14 = (f32[256,384]{1,0:T(8,128)S(1)}, f32[256,384]{1,0:T(8,128)S(1)}, u32[]{:S(2)}, u32[]{:S(2)}) collective-permute-start(f32[256,384]{1,0:T(8,128)S(1)} %get-tuple-element.441.refs_1_), channel_id=1, source_target_pairs={{8,0},{24,16},{16,24},{0,8},{9,1},{25,17},{17,25},{1,9},{10,2},{26... | collective-permute-start | bytes 1179656 | tf_op jit(solution)/shard_map/ppermute | solution.py:544
  234.9 1.4 collective-permute-start.15
  237.0 21.7 %collective-permute-start.16 = (f32[256,384]{1,0:T(8,128)S(1)}, f32[256,384]{1,0:T(8,128)S(1)}, u32[]{:S(2)}, u32[]{:S(2)}) collective-permute-start(f32[256,384]{1,0:T(8,128)S(1)} %get-tuple-element.467.refs_1_), channel_id=1, source_target_pairs={{8,0},{24,16},{16,24},{9,1},{25,17},{17,25},{10,2},{26,18},{18,26}... | collective-permute-start | bytes 1179656 | tf_op jit(solution)/shard_map/ppermute | solution.py:544
  262.5 12.8 %collective-permute-start.17 = (f32[256,384]{1,0:T(8,128)S(1)}, f32[256,384]{1,0:T(8,128)S(1)}, u32[]{:S(2)}, u32[]{:S(2)}) collective-permute-start(f32[256,384]{1,0:T(8,128)S(1)} %get-tuple-element.480.refs_1_), channel_id=1, source_target_pairs={{16,8},{17,9},{18,10},{19,11},{20,12},{21,13},{22,14},{23,15}} | collective-permute-start | bytes 1179656 | tf_op jit(solution)/shard_map/ppermute | solution.py:544
  265.0 14.3 %copy-start.6 = (f32[4,256,384]{2,1,0:T(8,128)S(1)}, f32[4,256,384]{2,1,0:T(8,128)}, u32[]{:S(2)}) copy-start(f32[4,256,384]{2,1,0:T(8,128)} %copy-done.5) | copy-start | bytes 4718596
  280.2 9.7 %collective-permute-start.18 = (f32[256,384]{1,0:T(8,128)S(1)}, f32[256,384]{1,0:T(8,128)S(1)}, u32[]{:S(2)}, u32[]{:S(2)}) collective-permute-start(f32[256,384]{1,0:T(8,128)S(1)} %get-tuple-element.493), channel_id=1, source_target_pairs={{8,0},{24,16},{9,1},{25,17},{10,2},{26,18},{11,3},{27,19},{12,4},{... | collective-permute-start | bytes 1179656 | tf_op jit(solution)/shard_map/ppermute | solution.py:544
  293.6 0.7 collective-permute-start.19
  295.0 25.5 %collective-permute-start.20 = (f32[256,384]{1,0:T(8,128)S(1)}, f32[256,384]{1,0:T(8,128)S(1)}, u32[]{:S(2)}, u32[]{:S(2)}) collective-permute-start(f32[256,384]{1,0:T(8,128)S(1)} %get-tuple-element.507), channel_id=1, source_target_pairs={{8,0},{9,1},{10,2},{11,3},{12,4},{13,5},{14,6},{15,7}} | collective-permute-start | bytes 1179656 | tf_op jit(solution)/shard_map/ppermute | solution.py:544
  333.6 172.9 %reduce-scatter.5.cloned.1.call-start = ((), (), s32[]{:S(2)}) async-start(), calls=%async_computation.3 | async-start | bytes 11943936 | tf_op jit(solution)/shard_map/reduce_scatter | solution.py:551
  (10 other events, 21.6 us)
Sparse Core Ops, SparseCore 0:
  333.8 60.7 reduce-scatter.2
  397.5 108.9 reduce-scatter.4
